TPU v7x, 32 devices: a whole 2x2x4 slice. The times are simulated.
32 devices in a mesh: shell: 4 (over z), sky: 8 (over y, x, core).
Axes of the slice: x: 2, y: 2, z: 4, core: 2. Of those that a mesh axis runs over, the one named last changes fastest.
Arguments:
- density: bfloat16 [100, 384, 384], P('shell', 'sky'), may hold values from -6 to 6
- kernel_table: float32 [16, 4], replicated, may hold values from 0.02 to 0.4
- shell_row: int32 [100], P('shell'), may hold values from 0 to 15, as said below
- theta_first: bfloat16 [6, 4, 64], replicated, may hold values from -1.25 to 1.25
- bias_first: float32 [64], replicated, may hold values from -3 to 3
- theta_second: bfloat16 [6, 64, 64], replicated, may hold values from -0.3125 to 0.3125
- bias_second: float32 [64], replicated, may hold values from -3 to 3
Outputs:
- features: bfloat16 [64, 384, 384], P('shell', 'sky')
Inputs may be any that keep to these rules, and one draw needn't show every extreme that they name: `shell_row`: each shell names one row of kernel_table; both the first and the last row are named.
All inputs are finite; a program needn't handle non-finite values.
Results may differ from a plain program's by a relative error of at most 0.0062.
Values may be sent and summed in bfloat16 or wider, within the bound.
A program may use at most 128 MiB of HBM per device.

v0:
```python
import jax
import jax.numpy as jnp
from jax import lax
from jax.sharding import PartitionSpec as P


def padded(block, sides, width):
    for axis, dim in sides:
        count = lax.axis_size(axis)
        forward = [(i, i + 1) for i in range(count - 1)]
        forward.append((count - 1, 0))
        backward = [(target, source) for source, target in forward]
        low = lax.ppermute(
            lax.slice_in_dim(block, block.shape[dim] - width, None, axis=dim), axis, forward
        )
        high = lax.ppermute(lax.slice_in_dim(block, 0, width, axis=dim), axis, backward)
        block = jnp.concatenate([low, block, high], axis=dim)
    return block


def lateral(source_field):
    right_side = jnp.pad(source_field[:, :, 1:], ((0, 0), (0, 0), (0, 1)))
    left_side = jnp.pad(source_field[:, :, :-1], ((0, 0), (0, 0), (1, 0)))
    return right_side + left_side


def apply_rows(extended):
    return -0.25 * (extended[:, :-2] + extended[:, 2:] + lateral(extended[:, 1:-1]))


def basis_of(source_field, is_first, degrees):
    collected = [source_field.astype(jnp.bfloat16)]
    earlier = source_field.astype(jnp.float32)
    current = earlier
    for degree in range(1, degrees):
        if is_first:
            extended = padded(current, (("sky", 1),), 1)
        else:
            extended = padded(current, (("sky", 1),), 1)
        mapped = apply_rows(extended)
        if degree == 1:
            following = mapped
        else:
            following = 2.0 * mapped - earlier
        earlier = current
        current = following
        collected.append(following.astype(jnp.bfloat16))
    return jnp.stack(collected)


def per_device(
    density, kernel_table, shell_row, theta_first, bias_first, theta_second, bias_second
):
    degrees = theta_first.shape[0]
    table_rows = kernel_table.shape[0]
    table_ids = lax.broadcasted_iota(jnp.int32, (shell_row.shape[0], table_rows), 1)
    selector = (shell_row[:, None] == table_ids).astype(jnp.float32)
    weights = jnp.dot(selector, kernel_table, precision=lax.Precision.HIGHEST).astype(jnp.bfloat16)
    partial_sum = jnp.einsum("sb,syx->byx", weights, density, preferred_element_type=jnp.float32)
    convergence = lax.psum(partial_sum, "shell")
    first_basis = basis_of(convergence, True, degrees)
    groups = lax.axis_size("shell")
    shell_index = lax.axis_index("shell")
    width_out = theta_second.shape[2] // groups
    out_start = shell_index * width_out
    hidden = jnp.einsum(
        "kbo,kbyx->oyx", theta_first, first_basis, preferred_element_type=jnp.float32
    )
    hidden = jnp.maximum(hidden + bias_first[:, None, None], 0.0).astype(jnp.bfloat16)
    second_basis = basis_of(hidden, False, degrees)
    theta_cols = lax.dynamic_slice_in_dim(theta_second, out_start, width_out, 2)
    summed = jnp.einsum(
        "kio,kiyx->oyx", theta_cols, second_basis, preferred_element_type=jnp.float32
    )
    bias_cols = lax.dynamic_slice_in_dim(bias_second, out_start, width_out, 0)
    return (summed + bias_cols[:, None, None]).astype(jnp.bfloat16)


def solution(mesh):
    return jax.shard_map(
        per_device,
        mesh=mesh,
        in_specs=(P("shell", "sky", None), P(), P("shell"), P(), P(), P(), P()),
        out_specs=P("shell", "sky", None),
        check_vma=False,
    )
```

profile of v0, /device:TPU:0, one launch (start us, length us, event | category | flops | bytes accessed | tf_op | source)
XLA Modules:
  0.0 148.8 jit_solution(16323545694625500989)
XLA Ops:
  7.7 1.0 fusion.24
  9.5 38.8 %all-reduce.22.cloned.1.call-done = f32[4,48,384]{2,0,1:T(4,128)} async-done(((f32[4,48,384]{2,0,1:T(4,128)}), f32[4,48,384]{2,0,1:T(4,128)}) %all-reduce.22.cloned.1.call-update) | async-done | bytes 294928 | tf_op jit(solution)/shard_map/psum | solution.py:60
  49.0 2.6 %collective-permute-start.1 = (f32[4,1,384]{2,0,1:T(4,128)S(1)}, f32[4,1,384]{2,0,1:T(4,128)S(1)}, u32[]{:S(2)}, u32[]{:S(2)}) collective-permute-start(f32[4,1,384]{2,0,1:T(4,128)S(1)} %get-tuple-element.58), channel_id=1, source_target_pairs={{1,0},{2,1},{3,2},{4,3},{5,4},{6,5},{7,6},{0,7},{9,8},{10,9},{11,1... | collective-permute-start | bytes 18440 | tf_op jit(solution)/shard_map/ppermute | solution.py:16
  51.7 1.3 fusion.79
  52.9 1.0 bitcast_dynamic-update-slice_fusion.11
  54.0 1.3 bitcast_dynamic-update-slice_fusion.10
  55.4 2.6 %collective-permute-start.3 = (f32[4,1,384]{2,0,1:T(4,128)S(1)}, f32[4,1,384]{2,0,1:T(4,128)S(1)}, u32[]{:S(2)}, u32[]{:S(2)}) collective-permute-start(f32[4,1,384]{2,0,1:T(4,128)S(1)} %get-tuple-element.54), channel_id=1, source_target_pairs={{1,0},{2,1},{3,2},{4,3},{5,4},{6,5},{7,6},{0,7},{9,8},{10,9},{11,1... | collective-permute-start | bytes 18440 | tf_op jit(solution)/shard_map/ppermute | solution.py:16
  58.2 1.1 collective-permute-done.2
  59.4 1.3 bitcast_dynamic-update-slice_fusion.9
  60.8 2.6 %collective-permute-start.5 = (f32[4,1,384]{2,0,1:T(4,128)S(1)}, f32[4,1,384]{2,0,1:T(4,128)S(1)}, u32[]{:S(2)}, u32[]{:S(2)}) collective-permute-start(f32[4,1,384]{2,0,1:T(4,128)S(1)} %get-tuple-element.50), channel_id=1, source_target_pairs={{1,0},{2,1},{3,2},{4,3},{5,4},{6,5},{7,6},{0,7},{9,8},{10,9},{11,1... | collective-permute-start | bytes 18440 | tf_op jit(solution)/shard_map/ppermute | solution.py:16
  63.6 1.1 collective-permute-done.4
  65.5 2.2 %collective-permute-start.7 = (f32[4,1,384]{2,0,1:T(4,128)S(1)}, f32[4,1,384]{2,0,1:T(4,128)S(1)}, u32[]{:S(2)}, u32[]{:S(2)}) collective-permute-start(f32[4,1,384]{2,0,1:T(4,128)S(1)} %get-tuple-element.46), channel_id=1, source_target_pairs={{1,0},{2,1},{3,2},{4,3},{5,4},{6,5},{7,6},{0,7},{9,8},{10,9},{11,1... | collective-permute-start | bytes 18440 | tf_op jit(solution)/shard_map/ppermute | solution.py:16
  67.9 1.1 collective-permute-done.6
  69.8 2.2 %collective-permute-start.9 = (f32[4,1,384]{2,0,1:T(4,128)S(1)}, f32[4,1,384]{2,0,1:T(4,128)S(1)}, u32[]{:S(2)}, u32[]{:S(2)}) collective-permute-start(f32[4,1,384]{2,0,1:T(4,128)S(1)} %get-tuple-element.42), channel_id=1, source_target_pairs={{1,0},{2,1},{3,2},{4,3},{5,4},{6,5},{7,6},{0,7},{9,8},{10,9},{11,1... | collective-permute-start | bytes 18440 | tf_op jit(solution)/shard_map/ppermute | solution.py:16
  72.3 1.1 collective-permute-done.8
  73.7 2.5 %bitcast_dynamic-update-slice_fusion = (bf16[6,64,48,384]{3,1,2,0:T(8,128)(2,1)}, bf16[48,384,64]{1,2,0:T(8,128)(2,1)S(1)}) fusion(f32[64]{0:T(128)S(1)} %copy-done.5, bf16[6,4,48,384]{3,1,2,0:T(4,128)(2,1)S(1)} %bitcast_dynamic-update-slice_fusion.6, bf16[6,4,64]{2,1,0:T(4,128)(2,1)S(1)} %copy-done.4), kind=kOutput, calls=%fused_computation.33 | convolution fusion | flops 60162048 | bytes 5606656 | tf_op jit(solution)/shard_map/kbo,kbyx->oyx/dot_general | solution.py:66
  77.6 2.6 %collective-permute-start.11 = (f32[64,1,384]{2,0,1:T(8,128)S(1)}, f32[64,1,384]{2,0,1:T(8,128)S(1)}, u32[]{:S(2)}, u32[]{:S(2)}) collective-permute-start(f32[64,1,384]{2,0,1:T(8,128)S(1)} %get-tuple-element.38), channel_id=1, source_target_pairs={{1,0},{2,1},{3,2},{4,3},{5,4},{6,5},{7,6},{0,7},{9,8},{10,9},{11,1... | collective-permute-start | bytes 294920 | tf_op jit(solution)/shard_map/ppermute | solution.py:16
  80.2 1.8 %fusion.69 = (f32[64,48,383]{2,0,1:T(8,128)S(1)}, f32[64,48,383]{2,0,1:T(8,128)S(1)}) fusion(f32[64,48,384]{2,0,1:T(8,128)S(1)} %bitcast_convert_fusion), kind=kLoop, calls=%fused_computation.98 | loop fusion | bytes 18825216 | tf_op jit(solution)/shard_map/slice | solution.py:22
  82.4 3.7 %bitcast_dynamic-update-slice_fusion.5 = (bf16[6,64,48,384]{3,1,2,0:T(8,128)(2,1)}, f32[64,48,384]{2,0,1:T(8,128)S(1)}) fusion(bf16[6,64,48,384]{3,1,2,0:T(8,128)(2,1)} %get-tuple-element.61, f32[64,48,383]{2,0,1:T(8,128)S(1)} %get-tuple-element.40, f32[64,48,383]{2,0,1:T(8,128)S(1)} %get-tuple-element.39, f32[64,1,384]{2,0,1:T(8,128)S(1)} %collective-permute-done.11, ...), kind=kLoop, calls=%fused_computation.38 | loop fusion | flops 8257536 | bytes 21405696
  86.5 2.5 %collective-permute-start.13 = (f32[64,1,384]{2,0,1:T(8,128)S(1)}, f32[64,1,384]{2,0,1:T(8,128)S(1)}, u32[]{:S(2)}, u32[]{:S(2)}) collective-permute-start(f32[64,1,384]{2,0,1:T(8,128)S(1)} %get-tuple-element.34), channel_id=1, source_target_pairs={{1,0},{2,1},{3,2},{4,3},{5,4},{6,5},{7,6},{0,7},{9,8},{10,9},{11,1... | collective-permute-start | bytes 294920 | tf_op jit(solution)/shard_map/ppermute | solution.py:16
  89.0 1.8 %fusion.67 = (f32[64,48,383]{2,0,1:T(8,128)S(1)}, f32[64,48,383]{2,0,1:T(8,128)S(1)}) fusion(f32[64,48,384]{2,0,1:T(8,128)S(1)} %get-tuple-element.12), kind=kLoop, calls=%fused_computation.96 | loop fusion | bytes 18825216 | tf_op jit(solution)/shard_map/slice | solution.py:22
  91.6 5.3 %bitcast_dynamic-update-slice_fusion.4 = (bf16[6,64,48,384]{3,1,2,0:T(8,128)(2,1)}, f32[64,48,384]{2,0,1:T(8,128)S(1)}) fusion(bf16[6,64,48,384]{3,1,2,0:T(8,128)(2,1)} %get-tuple-element.11, bf16[48,384,64]{1,2,0:T(8,128)(2,1)} %copy-done.2, f32[64,48,383]{2,0,1:T(8,128)S(1)} %get-tuple-element.36, f32[64,48,383]{2,0,1:T(8,128)S(1)} %get-tuple-element.35, ...), kind=kLoop, calls=%fused_computation.37 | loop fusion | flops 10616832 | bytes 23764992
  97.4 2.2 %collective-permute-start.15 = (f32[64,1,384]{2,0,1:T(8,128)S(1)}, f32[64,1,384]{2,0,1:T(8,128)S(1)}, u32[]{:S(2)}, u32[]{:S(2)}) collective-permute-start(f32[64,1,384]{2,0,1:T(8,128)S(1)} %get-tuple-element.30), channel_id=1, source_target_pairs={{1,0},{2,1},{3,2},{4,3},{5,4},{6,5},{7,6},{0,7},{9,8},{10,9},{11,1... | collective-permute-start | bytes 294920 | tf_op jit(solution)/shard_map/ppermute | solution.py:16
  99.6 3.8 %fusion.65 = (f32[64,48,383]{2,0,1:T(8,128)S(1)}, f32[64,48,383]{2,0,1:T(8,128)}) fusion(f32[64,48,384]{2,0,1:T(8,128)S(1)} %get-tuple-element.10), kind=kLoop, calls=%fused_computation.94 | loop fusion | bytes 18825216 | tf_op jit(solution)/shard_map/slice | solution.py:22
  103.4 5.9 %bitcast_dynamic-update-slice_fusion.3 = (bf16[6,64,48,384]{3,1,2,0:T(8,128)(2,1)}, f32[64,48,384]{2,0,1:T(8,128)S(1)}) fusion(bf16[6,64,48,384]{3,1,2,0:T(8,128)(2,1)} %get-tuple-element.9, f32[64,48,384]{2,0,1:T(8,128)S(1)} %get-tuple-element.12, f32[64,48,383]{2,0,1:T(8,128)} %get-tuple-element.32, f32[64,48,383]{2,0,1:T(8,128)S(1)} %get-tuple-element.31, ...), kind=kLoop, calls=%fused_computation.36 | loop fusion | flops 9437184 | bytes 26136576
  109.4 2.6 %collective-permute-start.17 = (f32[64,1,384]{2,0,1:T(8,128)S(1)}, f32[64,1,384]{2,0,1:T(8,128)S(1)}, u32[]{:S(2)}, u32[]{:S(2)}) collective-permute-start(f32[64,1,384]{2,0,1:T(8,128)S(1)} %get-tuple-element.26), channel_id=1, source_target_pairs={{1,0},{2,1},{3,2},{4,3},{5,4},{6,5},{7,6},{0,7},{9,8},{10,9},{11,1... | collective-permute-start | bytes 294920 | tf_op jit(solution)/shard_map/ppermute | solution.py:16
  112.1 3.8 %fusion.63 = (f32[64,48,383]{2,0,1:T(8,128)S(1)}, f32[64,48,383]{2,0,1:T(8,128)}) fusion(f32[64,48,384]{2,0,1:T(8,128)S(1)} %get-tuple-element.8), kind=kLoop, calls=%fused_computation.92 | loop fusion | bytes 18825216 | tf_op jit(solution)/shard_map/slice | solution.py:22
  115.9 5.8 %bitcast_dynamic-update-slice_fusion.2 = (bf16[6,64,48,384]{3,1,2,0:T(8,128)(2,1)}, f32[64,48,384]{2,0,1:T(8,128)S(1)}) fusion(bf16[6,64,48,384]{3,1,2,0:T(8,128)(2,1)} %get-tuple-element.7, f32[64,48,384]{2,0,1:T(8,128)S(1)} %get-tuple-element.10, f32[64,48,383]{2,0,1:T(8,128)} %get-tuple-element.28, f32[64,48,383]{2,0,1:T(8,128)S(1)} %get-tuple-element.27, ...), kind=kLoop, calls=%fused_computation.35 | loop fusion | flops 9437184 | bytes 26136576
  121.8 2.6 %collective-permute-start.19 = (f32[64,1,384]{2,0,1:T(8,128)S(1)}, f32[64,1,384]{2,0,1:T(8,128)S(1)}, u32[]{:S(2)}, u32[]{:S(2)}) collective-permute-start(f32[64,1,384]{2,0,1:T(8,128)S(1)} %get-tuple-element.22), channel_id=1, source_target_pairs={{1,0},{2,1},{3,2},{4,3},{5,4},{6,5},{7,6},{0,7},{9,8},{10,9},{11,1... | collective-permute-start | bytes 294920 | tf_op jit(solution)/shard_map/ppermute | solution.py:16
  124.4 3.8 %fusion.61 = (f32[64,48,383]{2,0,1:T(8,128)S(1)}, f32[64,48,383]{2,0,1:T(8,128)}) fusion(f32[64,48,384]{2,0,1:T(8,128)S(1)} %get-tuple-element.6), kind=kLoop, calls=%fused_computation.90 | loop fusion | bytes 18825216 | tf_op jit(solution)/shard_map/slice | solution.py:22
  128.2 5.7 %bitcast_dynamic-update-slice_fusion.1 = bf16[6,64,48,384]{3,1,2,0:T(8,128)(2,1)} fusion(bf16[6,64,48,384]{3,1,2,0:T(8,128)(2,1)} %get-tuple-element.5, f32[64,48,384]{2,0,1:T(8,128)S(1)} %get-tuple-element.8, f32[64,48,383]{2,0,1:T(8,128)} %get-tuple-element.24, f32[64,48,383]{2,0,1:T(8,128)S(1)} %get-tuple-element.23, ...), kind=kLoop, calls=%fused_computation.34 | loop fusion | flops 9437184 | bytes 21417984 | tf_op jit(solution)/shard_map/stack | solution.py:48
  133.9 7.1 %fusion.23 = bf16[16,48,384]{2,0,1:T(8,128)(2,1)S(1)} fusion(bf16[6,64,48,384]{3,1,2,0:T(8,128)(2,1)} %bitcast_dynamic-update-slice_fusion.1, f32[16]{0:T(128)S(1)} %dynamic_slice.7, bf16[6,64,64]{2,1,0:T(8,128)(2,1)S(1)} %copy-done.3, s32[]{:T(128)S(6)} %select_n.4), kind=kOutput, calls=%fused_computation.42 | convolution fusion | flops 227082240 | bytes 14794820 | tf_op jit(solution)/shard_map/kio,kiyx->oyx/dot_general | solution.py:72
  (61 shorter events, 10.3 us)
Async XLA Ops:
  6.5 1.2 copy-start
  6.5 41.8 %all-reduce.22.cloned.1.call-start = ((), (), s32[]{:S(2)}) async-start(), calls=%async_computation | async-start | bytes 589824 | tf_op jit(solution)/shard_map/psum | solution.py:60
  49.0 4.9 %collective-permute-start = (f32[4,1,384]{2,0,1:T(4,128)S(1)}, f32[4,1,384]{2,0,1:T(4,128)S(1)}, u32[]{:S(2)}, u32[]{:S(2)}) collective-permute-start(f32[4,1,384]{2,0,1:T(4,128)S(1)} %get-tuple-element.57), channel_id=1, source_target_pairs={{0,1},{1,2},{2,3},{3,4},{4,5},{5,6},{6,7},{7,0},{8,9},{9,10},{10,1... | collective-permute-start | bytes 18440 | tf_op jit(solution)/shard_map/ppermute | solution.py:13
  49.0 4.9 %collective-permute-start.1 = (f32[4,1,384]{2,0,1:T(4,128)S(1)}, f32[4,1,384]{2,0,1:T(4,128)S(1)}, u32[]{:S(2)}, u32[]{:S(2)}) collective-permute-start(f32[4,1,384]{2,0,1:T(4,128)S(1)} %get-tuple-element.58), channel_id=1, source_target_pairs={{1,0},{2,1},{3,2},{4,3},{5,4},{6,5},{7,6},{0,7},{9,8},{10,9},{11,1... | collective-permute-start | bytes 18440 | tf_op jit(solution)/shard_map/ppermute | solution.py:16
  55.3 4.0 %collective-permute-start.2 = (f32[4,1,384]{2,0,1:T(4,128)S(1)}, f32[4,1,384]{2,0,1:T(4,128)S(1)}, u32[]{:S(2)}, u32[]{:S(2)}) collective-permute-start(f32[4,1,384]{2,0,1:T(4,128)S(1)} %get-tuple-element.53), channel_id=1, source_target_pairs={{0,1},{1,2},{2,3},{3,4},{4,5},{5,6},{6,7},{7,0},{8,9},{9,10},{10,1... | collective-permute-start | bytes 18440 | tf_op jit(solution)/shard_map/ppermute | solution.py:13
  55.4 4.0 %collective-permute-start.3 = (f32[4,1,384]{2,0,1:T(4,128)S(1)}, f32[4,1,384]{2,0,1:T(4,128)S(1)}, u32[]{:S(2)}, u32[]{:S(2)}) collective-permute-start(f32[4,1,384]{2,0,1:T(4,128)S(1)} %get-tuple-element.54), channel_id=1, source_target_pairs={{1,0},{2,1},{3,2},{4,3},{5,4},{6,5},{7,6},{0,7},{9,8},{10,9},{11,1... | collective-permute-start | bytes 18440 | tf_op jit(solution)/shard_map/ppermute | solution.py:16
  59.4 14.3 %copy-start.4 = (bf16[6,4,64]{2,1,0:T(4,128)(2,1)S(1)}, bf16[6,4,64]{2,1,0:T(4,128)(2,1)}, u32[]{:S(2)}) copy-start(bf16[6,4,64]{2,1,0:T(4,128)(2,1)} %param.10) | copy-start | bytes 9220
  59.4 14.3 %copy-start.5 = (f32[64]{0:T(128)S(1)}, f32[64]{0:T(128)}, u32[]{:S(2)}) copy-start(f32[64]{0:T(128)} %param.11) | copy-start | bytes 772
  60.6 4.0 %collective-permute-start.4 = (f32[4,1,384]{2,0,1:T(4,128)S(1)}, f32[4,1,384]{2,0,1:T(4,128)S(1)}, u32[]{:S(2)}, u32[]{:S(2)}) collective-permute-start(f32[4,1,384]{2,0,1:T(4,128)S(1)} %get-tuple-element.49), channel_id=1, source_target_pairs={{0,1},{1,2},{2,3},{3,4},{4,5},{5,6},{6,7},{7,0},{8,9},{9,10},{10,1... | collective-permute-start | bytes 18440 | tf_op jit(solution)/shard_map/ppermute | solution.py:13
  60.8 4.0 %collective-permute-start.5 = (f32[4,1,384]{2,0,1:T(4,128)S(1)}, f32[4,1,384]{2,0,1:T(4,128)S(1)}, u32[]{:S(2)}, u32[]{:S(2)}) collective-permute-start(f32[4,1,384]{2,0,1:T(4,128)S(1)} %get-tuple-element.50), channel_id=1, source_target_pairs={{1,0},{2,1},{3,2},{4,3},{5,4},{6,5},{7,6},{0,7},{9,8},{10,9},{11,1... | collective-permute-start | bytes 18440 | tf_op jit(solution)/shard_map/ppermute | solution.py:16
  65.0 4.0 %collective-permute-start.6 = (f32[4,1,384]{2,0,1:T(4,128)S(1)}, f32[4,1,384]{2,0,1:T(4,128)S(1)}, u32[]{:S(2)}, u32[]{:S(2)}) collective-permute-start(f32[4,1,384]{2,0,1:T(4,128)S(1)} %get-tuple-element.45), channel_id=1, source_target_pairs={{0,1},{1,2},{2,3},{3,4},{4,5},{5,6},{6,7},{7,0},{8,9},{9,10},{10,1... | collective-permute-start | bytes 18440 | tf_op jit(solution)/shard_map/ppermute | solution.py:13
  65.5 3.6 %collective-permute-start.7 = (f32[4,1,384]{2,0,1:T(4,128)S(1)}, f32[4,1,384]{2,0,1:T(4,128)S(1)}, u32[]{:S(2)}, u32[]{:S(2)}) collective-permute-start(f32[4,1,384]{2,0,1:T(4,128)S(1)} %get-tuple-element.46), channel_id=1, source_target_pairs={{1,0},{2,1},{3,2},{4,3},{5,4},{6,5},{7,6},{0,7},{9,8},{10,9},{11,1... | collective-permute-start | bytes 18440 | tf_op jit(solution)/shard_map/ppermute | solution.py:16
  69.4 4.0 %collective-permute-start.8 = (f32[4,1,384]{2,0,1:T(4,128)S(1)}, f32[4,1,384]{2,0,1:T(4,128)S(1)}, u32[]{:S(2)}, u32[]{:S(2)}) collective-permute-start(f32[4,1,384]{2,0,1:T(4,128)S(1)} %get-tuple-element.41), channel_id=1, source_target_pairs={{0,1},{1,2},{2,3},{3,4},{4,5},{5,6},{6,7},{7,0},{8,9},{9,10},{10,1... | collective-permute-start | bytes 18440 | tf_op jit(solution)/shard_map/ppermute | solution.py:13
  69.8 3.6 %collective-permute-start.9 = (f32[4,1,384]{2,0,1:T(4,128)S(1)}, f32[4,1,384]{2,0,1:T(4,128)S(1)}, u32[]{:S(2)}, u32[]{:S(2)}) collective-permute-start(f32[4,1,384]{2,0,1:T(4,128)S(1)} %get-tuple-element.42), channel_id=1, source_target_pairs={{1,0},{2,1},{3,2},{4,3},{5,4},{6,5},{7,6},{0,7},{9,8},{10,9},{11,1... | collective-permute-start | bytes 18440 | tf_op jit(solution)/shard_map/ppermute | solution.py:16
  76.2 1.4 copy-start.2
  76.8 5.4 %collective-permute-start.10 = (f32[64,1,384]{2,0,1:T(8,128)S(1)}, f32[64,1,384]{2,0,1:T(8,128)S(1)}, u32[]{:S(2)}, u32[]{:S(2)}) collective-permute-start(f32[64,1,384]{2,0,1:T(8,128)S(1)} %get-tuple-element.37), channel_id=1, source_target_pairs={{0,1},{1,2},{2,3},{3,4},{4,5},{5,6},{6,7},{7,0},{8,9},{9,10},{10,1... | collective-permute-start | bytes 294920 | tf_op jit(solution)/shard_map/ppermute | solution.py:13
  77.6 4.8 %collective-permute-start.11 = (f32[64,1,384]{2,0,1:T(8,128)S(1)}, f32[64,1,384]{2,0,1:T(8,128)S(1)}, u32[]{:S(2)}, u32[]{:S(2)}) collective-permute-start(f32[64,1,384]{2,0,1:T(8,128)S(1)} %get-tuple-element.38), channel_id=1, source_target_pairs={{1,0},{2,1},{3,2},{4,3},{5,4},{6,5},{7,6},{0,7},{9,8},{10,9},{11,1... | collective-permute-start | bytes 294920 | tf_op jit(solution)/shard_map/ppermute | solution.py:16
  86.1 5.5 %collective-permute-start.12 = (f32[64,1,384]{2,0,1:T(8,128)S(1)}, f32[64,1,384]{2,0,1:T(8,128)S(1)}, u32[]{:S(2)}, u32[]{:S(2)}) collective-permute-start(f32[64,1,384]{2,0,1:T(8,128)S(1)} %get-tuple-element.33), channel_id=1, source_target_pairs={{0,1},{1,2},{2,3},{3,4},{4,5},{5,6},{6,7},{7,0},{8,9},{9,10},{10,1... | collective-permute-start | bytes 294920 | tf_op jit(solution)/shard_map/ppermute | solution.py:13
  86.5 5.1 %collective-permute-start.13 = (f32[64,1,384]{2,0,1:T(8,128)S(1)}, f32[64,1,384]{2,0,1:T(8,128)S(1)}, u32[]{:S(2)}, u32[]{:S(2)}) collective-permute-start(f32[64,1,384]{2,0,1:T(8,128)S(1)} %get-tuple-element.34), channel_id=1, source_target_pairs={{1,0},{2,1},{3,2},{4,3},{5,4},{6,5},{7,6},{0,7},{9,8},{10,9},{11,1... | collective-permute-start | bytes 294920 | tf_op jit(solution)/shard_map/ppermute | solution.py:16
  96.9 6.5 %collective-permute-start.14 = (f32[64,1,384]{2,0,1:T(8,128)S(1)}, f32[64,1,384]{2,0,1:T(8,128)S(1)}, u32[]{:S(2)}, u32[]{:S(2)}) collective-permute-start(f32[64,1,384]{2,0,1:T(8,128)S(1)} %get-tuple-element.29), channel_id=1, source_target_pairs={{0,1},{1,2},{2,3},{3,4},{4,5},{5,6},{6,7},{7,0},{8,9},{9,10},{10,1... | collective-permute-start | bytes 294920 | tf_op jit(solution)/shard_map/ppermute | solution.py:13
  97.4 6.0 %collective-permute-start.15 = (f32[64,1,384]{2,0,1:T(8,128)S(1)}, f32[64,1,384]{2,0,1:T(8,128)S(1)}, u32[]{:S(2)}, u32[]{:S(2)}) collective-permute-start(f32[64,1,384]{2,0,1:T(8,128)S(1)} %get-tuple-element.30), channel_id=1, source_target_pairs={{1,0},{2,1},{3,2},{4,3},{5,4},{6,5},{7,6},{0,7},{9,8},{10,9},{11,1... | collective-permute-start | bytes 294920 | tf_op jit(solution)/shard_map/ppermute | solution.py:16
  109.4 6.5 %collective-permute-start.16 = (f32[64,1,384]{2,0,1:T(8,128)S(1)}, f32[64,1,384]{2,0,1:T(8,128)S(1)}, u32[]{:S(2)}, u32[]{:S(2)}) collective-permute-start(f32[64,1,384]{2,0,1:T(8,128)S(1)} %get-tuple-element.25), channel_id=1, source_target_pairs={{0,1},{1,2},{2,3},{3,4},{4,5},{5,6},{6,7},{7,0},{8,9},{9,10},{10,1... | collective-permute-start | bytes 294920 | tf_op jit(solution)/shard_map/ppermute | solution.py:13
  109.4 6.4 %collective-permute-start.17 = (f32[64,1,384]{2,0,1:T(8,128)S(1)}, f32[64,1,384]{2,0,1:T(8,128)S(1)}, u32[]{:S(2)}, u32[]{:S(2)}) collective-permute-start(f32[64,1,384]{2,0,1:T(8,128)S(1)} %get-tuple-element.26), channel_id=1, source_target_pairs={{1,0},{2,1},{3,2},{4,3},{5,4},{6,5},{7,6},{0,7},{9,8},{10,9},{11,1... | collective-permute-start | bytes 294920 | tf_op jit(solution)/shard_map/ppermute | solution.py:16
  121.7 6.5 %collective-permute-start.18 = (f32[64,1,384]{2,0,1:T(8,128)S(1)}, f32[64,1,384]{2,0,1:T(8,128)S(1)}, u32[]{:S(2)}, u32[]{:S(2)}) collective-permute-start(f32[64,1,384]{2,0,1:T(8,128)S(1)} %get-tuple-element.21), channel_id=1, source_target_pairs={{0,1},{1,2},{2,3},{3,4},{4,5},{5,6},{6,7},{7,0},{8,9},{9,10},{10,1... | collective-permute-start | bytes 294920 | tf_op jit(solution)/shard_map/ppermute | solution.py:13
  121.8 6.4 %collective-permute-start.19 = (f32[64,1,384]{2,0,1:T(8,128)S(1)}, f32[64,1,384]{2,0,1:T(8,128)S(1)}, u32[]{:S(2)}, u32[]{:S(2)}) collective-permute-start(f32[64,1,384]{2,0,1:T(8,128)S(1)} %get-tuple-element.22), channel_id=1, source_target_pairs={{1,0},{2,1},{3,2},{4,3},{5,4},{6,5},{7,6},{0,7},{9,8},{10,9},{11,1... | collective-permute-start | bytes 294920 | tf_op jit(solution)/shard_map/ppermute | solution.py:16
  128.2 5.8 %copy-start.3 = (bf16[6,64,64]{2,1,0:T(8,128)(2,1)S(1)}, bf16[6,64,64]{2,1,0:T(8,128)(2,1)}, u32[]{:S(2)}) copy-start(bf16[6,64,64]{2,1,0:T(8,128)(2,1)} %param.12) | copy-start | bytes 147460
  128.2 13.7 %copy-start.1 = (bf16[25,48,384]{2,1,0:T(8,128)(2,1)S(1)}, bf16[25,48,384]{2,1,0:T(8,128)(2,1)}, u32[]{:S(2)}) copy-start(bf16[25,48,384]{2,1,0:T(8,128)(2,1)} %param.7) | copy-start | bytes 2764804
Sparse Core Ops, SparseCore 0:
  9.7 38.5 all-reduce.21
where the time goes:
time: 149 us
  waiting for transfers between devices  44.6 us (30%)
  other arithmetic  31.4 us (21%)
  starting transfers between devices  27.5 us (18%)
  local copies, waits for them, and re-layouts  20.1 us (13%)
  between operations  13.6 us (9%)
  matrix products  11.5 us (8%)
    psum x1, waiting for transfers between devices, per_device(): convergence = lax.psum(partial_sum, 'shell')  38.8 us
    ppermute x10, starting transfers between devices, padded(): lax.ppermute(lax.slice_in_dim(block, 0, width, axis=dim), axis, backward)  24.9 us
    unnamed x9, other arithmetic  24.8 us
    slice x10, local copies, waits for them, and re-layouts, lateral(): right_side = jnp.pad(source_field[:, :, 1:], ((0, 0), (0, 0), (0, 1)))  17.1 us
    dot_general x1, matrix products, per_device(): jnp.einsum('kio,kiyx->oyx', theta_cols, second_basis, preferred_element_t...  7.06 us
    another operation x2, other arithmetic, basis_of(): return jnp.stack(collected)  5.99 us
    ppermute x10, waiting for transfers between devices, padded(): lax.ppermute(lax.slice_in_dim(block, block.shape[dim] - width, None, axis...  5.37 us
  transfers between devices with their start and end apart: 21, of which 11 were waited for; matrix products, arithmetic and copies ran while one was open for 13% of the time, Pallas kernels for 0%

commit v1 on v0

--- a/solution.py
+++ b/solution.py
@@ -57,7 +57,7 @@
     selector = (shell_row[:, None] == table_ids).astype(jnp.float32)
     weights = jnp.dot(selector, kernel_table, precision=lax.Precision.HIGHEST).astype(jnp.bfloat16)
     partial_sum = jnp.einsum("sb,syx->byx", weights, density, preferred_element_type=jnp.float32)
-    convergence = lax.psum(partial_sum, "shell")
+    convergence = jnp.sum(lax.all_gather(partial_sum, "shell"), axis=0)
     first_basis = basis_of(convergence, True, degrees)
     groups = lax.axis_size("shell")
     shell_index = lax.axis_index("shell")

time: 149 us -> 145 us (0.973)
  waiting for transfers between devices: 44.6 us -> 38 us
  local copies, waits for them, and re-layouts: 20.1 us -> 24.7 us
  other arithmetic: 31.4 us -> 29.7 us
    psum x1 -> x0, waiting for transfers between devices: 38.8 us -> none  [per_device(): convergence = lax.psum(partial_sum, 'shell')]
    all_gather x0 -> x1, waiting for transfers between devices: none -> 32.6 us  [per_device(): convergence = jnp.sum(lax.all_gather(partial_sum, 'shell'), axis=0)]
    another operation x0 -> x6, local copies, waits for them, and re-layouts: none -> 5.16 us  [basis_of(): return jnp.stack(collected)]
    unnamed x9 -> x4, other arithmetic: 24.8 us -> 20.7 us
    another operation x2 -> x6, other arithmetic: 5.99 us -> 7.01 us  [basis_of(): return jnp.stack(collected)]
  transfers between devices with their start and end apart: 21 -> 21, of which waited for: 11 -> 13; matrix products, arithmetic and copies ran while one was open for 13% -> 12% of each run, Pallas kernels for 0% -> 0%
where the time goes in v1:
time: 145 us
  waiting for transfers between devices  38 us (26%)
  other arithmetic  29.7 us (20%)
  starting transfers between devices  27.8 us (19%)
  local copies, waits for them, and re-layouts  24.7 us (17%)
  between operations  13.7 us (9%)
  matrix products  10.7 us (7%)
    all_gather x1, waiting for transfers between devices, per_device(): convergence = jnp.sum(lax.all_gather(partial_sum, 'shell'), axis=0)  32.6 us
    ppermute x10, starting transfers between devices, padded(): lax.ppermute(lax.slice_in_dim(block, 0, width, axis=dim), axis, backward)  24.2 us
    unnamed x4, other arithmetic  20.7 us
    slice x10, local copies, waits for them, and re-layouts, lateral(): right_side = jnp.pad(source_field[:, :, 1:], ((0, 0), (0, 0), (0, 1)))  16.1 us
    dot_general x1, matrix products, per_device(): jnp.einsum('kio,kiyx->oyx', theta_cols, second_basis, preferred_element_t...  7.06 us
    another operation x6, other arithmetic, basis_of(): return jnp.stack(collected)  7.01 us
    another operation x6, local copies, waits for them, and re-layouts, basis_of(): return jnp.stack(collected)  5.16 us
    ppermute x10, waiting for transfers between devices, padded(): lax.ppermute(lax.slice_in_dim(block, block.shape[dim] - width, None, axis...  4.91 us
  transfers between devices with their start and end apart: 21, of which 13 were waited for; matrix products, arithmetic and copies ran while one was open for 12% of the time, Pallas kernels for 0%

profile of v1, /device:TPU:0, one launch (start us, length us, event | category | flops | bytes accessed | tf_op | source)
XLA Modules:
  0.0 144.6 jit_solution(18071467632210101399)
XLA Ops:
  6.5 1.0 fusion.26
  8.0 0.7 copy.96
  9.5 32.6 %all-gather.3.cloned.1.call-done = f32[16,48,384]{2,1,0:T(8,128)} async-done(((f32[4,48,384]{2,1,0:T(8,128)}), f32[16,48,384]{2,1,0:T(8,128)}) %all-gather.3.cloned.1.call-update) | async-done | bytes 1179664 | tf_op jit(solution)/shard_map/all_gather | solution.py:60
  42.1 1.4 reduce_sum.9
  43.7 2.6 %collective-permute-start.1 = (f32[4,1,384]{2,0,1:T(4,128)S(1)}, f32[4,1,384]{2,0,1:T(4,128)S(1)}, u32[]{:S(2)}, u32[]{:S(2)}) collective-permute-start(f32[4,1,384]{2,0,1:T(4,128)S(1)} %get-tuple-element.58), channel_id=1, source_target_pairs={{1,0},{2,1},{3,2},{4,3},{5,4},{6,5},{7,6},{0,7},{9,8},{10,9},{11,1... | collective-permute-start | bytes 18440 | tf_op jit(solution)/shard_map/ppermute | solution.py:16
  48.6 2.0 %collective-permute-start.3 = (f32[4,1,384]{2,0,1:T(4,128)S(1)}, f32[4,1,384]{2,0,1:T(4,128)S(1)}, u32[]{:S(2)}, u32[]{:S(2)}) collective-permute-start(f32[4,1,384]{2,0,1:T(4,128)S(1)} %get-tuple-element.54), channel_id=1, source_target_pairs={{1,0},{2,1},{3,2},{4,3},{5,4},{6,5},{7,6},{0,7},{9,8},{10,9},{11,1... | collective-permute-start | bytes 18440 | tf_op jit(solution)/shard_map/ppermute | solution.py:16
  51.1 0.8 collective-permute-done.2
  52.8 2.2 %collective-permute-start.5 = (f32[4,1,384]{2,0,1:T(4,128)S(1)}, f32[4,1,384]{2,0,1:T(4,128)S(1)}, u32[]{:S(2)}, u32[]{:S(2)}) collective-permute-start(f32[4,1,384]{2,0,1:T(4,128)S(1)} %get-tuple-element.50), channel_id=1, source_target_pairs={{1,0},{2,1},{3,2},{4,3},{5,4},{6,5},{7,6},{0,7},{9,8},{10,9},{11,1... | collective-permute-start | bytes 18440 | tf_op jit(solution)/shard_map/ppermute | solution.py:16
  55.5 0.8 collective-permute-done.4
  57.1 2.3 %collective-permute-start.7 = (f32[4,1,384]{2,0,1:T(4,128)S(1)}, f32[4,1,384]{2,0,1:T(4,128)S(1)}, u32[]{:S(2)}, u32[]{:S(2)}) collective-permute-start(f32[4,1,384]{2,0,1:T(4,128)S(1)} %get-tuple-element.46), channel_id=1, source_target_pairs={{1,0},{2,1},{3,2},{4,3},{5,4},{6,5},{7,6},{0,7},{9,8},{10,9},{11,1... | collective-permute-start | bytes 18440 | tf_op jit(solution)/shard_map/ppermute | solution.py:16
  59.9 0.8 collective-permute-done.6
  61.5 2.3 %collective-permute-start.9 = (f32[4,1,384]{2,0,1:T(4,128)S(1)}, f32[4,1,384]{2,0,1:T(4,128)S(1)}, u32[]{:S(2)}, u32[]{:S(2)}) collective-permute-start(f32[4,1,384]{2,0,1:T(4,128)S(1)} %get-tuple-element.42), channel_id=1, source_target_pairs={{1,0},{2,1},{3,2},{4,3},{5,4},{6,5},{7,6},{0,7},{9,8},{10,9},{11,1... | collective-permute-start | bytes 18440 | tf_op jit(solution)/shard_map/ppermute | solution.py:16
  64.2 0.8 collective-permute-done.8
  65.6 4.0 %stack.45 = bf16[6,4,48,384]{3,0,1,2:T(8,128)(2,1)S(1)} concatenate(bf16[1,4,48,384]{3,0,1,2:T(2,128)(2,1)S(1)} %copy.104, bf16[1,4,48,384]{3,0,1,2:T(2,128)(2,1)S(1)} %copy.105, bf16[1,4,48,384]{3,0,1,2:T(2,128)(2,1)S(1)} %copy.106, bf16[1,4,48,384]{3,0,1,2:T(2,128)(2,1)S(1)} %copy.107, bf16[1,4,48,384]{3,0,1,2:T(2,128)(2,1)S(1)} %copy.108, bf16[1,4,48,384]{3,0,1,2:T(2,128)(2,1)S(1)} %copy.109), dimensions={0} | concatenate | bytes 1769472 | tf_op jit(solution)/shard_map/stack | solution.py:48
  69.6 2.4 %bitcast_dynamic-update-slice_fusion = (bf16[6,64,48,384]{3,1,2,0:T(8,128)(2,1)}, bf16[48,384,64]{1,2,0:T(8,128)(2,1)S(1)}) fusion(f32[64]{0:T(128)S(1)} %copy-done.5, bf16[6,4,48,384]{3,0,1,2:T(8,128)(2,1)S(1)} %stack.45, bf16[6,4,64]{2,1,0:T(4,128)(2,1)S(1)} %copy-done.4), kind=kOutput, calls=%fused_computation.33 | convolution fusion | flops 60162048 | bytes 5606656 | tf_op jit(solution)/shard_map/kbo,kbyx->oyx/dot_general | solution.py:66
  73.4 2.6 %collective-permute-start.11 = (f32[64,1,384]{2,0,1:T(8,128)S(1)}, f32[64,1,384]{2,0,1:T(8,128)S(1)}, u32[]{:S(2)}, u32[]{:S(2)}) collective-permute-start(f32[64,1,384]{2,0,1:T(8,128)S(1)} %get-tuple-element.38), channel_id=1, source_target_pairs={{1,0},{2,1},{3,2},{4,3},{5,4},{6,5},{7,6},{0,7},{9,8},{10,9},{11,1... | collective-permute-start | bytes 294920 | tf_op jit(solution)/shard_map/ppermute | solution.py:16
  76.0 1.8 %fusion.71 = (f32[64,48,383]{2,0,1:T(8,128)S(1)}, f32[64,48,383]{2,0,1:T(8,128)S(1)}) fusion(f32[64,48,384]{2,0,1:T(8,128)S(1)} %bitcast_convert_fusion), kind=kLoop, calls=%fused_computation.99 | loop fusion | bytes 18825216 | tf_op jit(solution)/shard_map/slice | solution.py:22
  78.2 3.7 %bitcast_dynamic-update-slice_fusion.5 = (bf16[6,64,48,384]{3,1,2,0:T(8,128)(2,1)}, f32[64,48,384]{2,0,1:T(8,128)S(1)}) fusion(bf16[6,64,48,384]{3,1,2,0:T(8,128)(2,1)} %get-tuple-element.61, f32[64,48,383]{2,0,1:T(8,128)S(1)} %get-tuple-element.40, f32[64,48,383]{2,0,1:T(8,128)S(1)} %get-tuple-element.39, f32[64,1,384]{2,0,1:T(8,128)S(1)} %collective-permute-done.11, ...), kind=kLoop, calls=%fused_computation.38 | loop fusion | flops 8257536 | bytes 21405696
  82.3 2.7 %collective-permute-start.13 = (f32[64,1,384]{2,0,1:T(8,128)S(1)}, f32[64,1,384]{2,0,1:T(8,128)S(1)}, u32[]{:S(2)}, u32[]{:S(2)}) collective-permute-start(f32[64,1,384]{2,0,1:T(8,128)S(1)} %get-tuple-element.34), channel_id=1, source_target_pairs={{1,0},{2,1},{3,2},{4,3},{5,4},{6,5},{7,6},{0,7},{9,8},{10,9},{11,1... | collective-permute-start | bytes 294920 | tf_op jit(solution)/shard_map/ppermute | solution.py:16
  85.0 1.8 %fusion.69 = (f32[64,48,383]{2,0,1:T(8,128)S(1)}, f32[64,48,383]{2,0,1:T(8,128)S(1)}) fusion(f32[64,48,384]{2,0,1:T(8,128)S(1)} %get-tuple-element.12), kind=kLoop, calls=%fused_computation.97 | loop fusion | bytes 18825216 | tf_op jit(solution)/shard_map/slice | solution.py:22
  87.4 5.3 %bitcast_dynamic-update-slice_fusion.4 = (bf16[6,64,48,384]{3,1,2,0:T(8,128)(2,1)}, f32[64,48,384]{2,0,1:T(8,128)S(1)}) fusion(bf16[6,64,48,384]{3,1,2,0:T(8,128)(2,1)} %get-tuple-element.11, bf16[48,384,64]{1,2,0:T(8,128)(2,1)} %copy-done.2, f32[64,48,383]{2,0,1:T(8,128)S(1)} %get-tuple-element.36, f32[64,48,383]{2,0,1:T(8,128)S(1)} %get-tuple-element.35, ...), kind=kLoop, calls=%fused_computation.37 | loop fusion | flops 10616832 | bytes 23764992
  93.2 2.2 %collective-permute-start.15 = (f32[64,1,384]{2,0,1:T(8,128)S(1)}, f32[64,1,384]{2,0,1:T(8,128)S(1)}, u32[]{:S(2)}, u32[]{:S(2)}) collective-permute-start(f32[64,1,384]{2,0,1:T(8,128)S(1)} %get-tuple-element.30), channel_id=1, source_target_pairs={{1,0},{2,1},{3,2},{4,3},{5,4},{6,5},{7,6},{0,7},{9,8},{10,9},{11,1... | collective-permute-start | bytes 294920 | tf_op jit(solution)/shard_map/ppermute | solution.py:16
  95.4 3.8 %fusion.67 = (f32[64,48,383]{2,0,1:T(8,128)S(1)}, f32[64,48,383]{2,0,1:T(8,128)}) fusion(f32[64,48,384]{2,0,1:T(8,128)S(1)} %get-tuple-element.10), kind=kLoop, calls=%fused_computation.95 | loop fusion | bytes 18825216 | tf_op jit(solution)/shard_map/slice | solution.py:22
  99.2 5.9 %bitcast_dynamic-update-slice_fusion.3 = (bf16[6,64,48,384]{3,1,2,0:T(8,128)(2,1)}, f32[64,48,384]{2,0,1:T(8,128)S(1)}) fusion(bf16[6,64,48,384]{3,1,2,0:T(8,128)(2,1)} %get-tuple-element.9, f32[64,48,384]{2,0,1:T(8,128)S(1)} %get-tuple-element.12, f32[64,48,383]{2,0,1:T(8,128)} %get-tuple-element.32, f32[64,48,383]{2,0,1:T(8,128)S(1)} %get-tuple-element.31, ...), kind=kLoop, calls=%fused_computation.36 | loop fusion | flops 9437184 | bytes 26136576
  105.2 2.6 %collective-permute-start.17 = (f32[64,1,384]{2,0,1:T(8,128)S(1)}, f32[64,1,384]{2,0,1:T(8,128)S(1)}, u32[]{:S(2)}, u32[]{:S(2)}) collective-permute-start(f32[64,1,384]{2,0,1:T(8,128)S(1)} %get-tuple-element.26), channel_id=1, source_target_pairs={{1,0},{2,1},{3,2},{4,3},{5,4},{6,5},{7,6},{0,7},{9,8},{10,9},{11,1... | collective-permute-start | bytes 294920 | tf_op jit(solution)/shard_map/ppermute | solution.py:16
  107.9 3.8 %fusion.65 = (f32[64,48,383]{2,0,1:T(8,128)S(1)}, f32[64,48,383]{2,0,1:T(8,128)}) fusion(f32[64,48,384]{2,0,1:T(8,128)S(1)} %get-tuple-element.8), kind=kLoop, calls=%fused_computation.93 | loop fusion | bytes 18825216 | tf_op jit(solution)/shard_map/slice | solution.py:22
  111.7 5.8 %bitcast_dynamic-update-slice_fusion.2 = (bf16[6,64,48,384]{3,1,2,0:T(8,128)(2,1)}, f32[64,48,384]{2,0,1:T(8,128)S(1)}) fusion(bf16[6,64,48,384]{3,1,2,0:T(8,128)(2,1)} %get-tuple-element.7, f32[64,48,384]{2,0,1:T(8,128)S(1)} %get-tuple-element.10, f32[64,48,383]{2,0,1:T(8,128)} %get-tuple-element.28, f32[64,48,383]{2,0,1:T(8,128)S(1)} %get-tuple-element.27, ...), kind=kLoop, calls=%fused_computation.35 | loop fusion | flops 9437184 | bytes 26136576
  117.6 2.6 %collective-permute-start.19 = (f32[64,1,384]{2,0,1:T(8,128)S(1)}, f32[64,1,384]{2,0,1:T(8,128)S(1)}, u32[]{:S(2)}, u32[]{:S(2)}) collective-permute-start(f32[64,1,384]{2,0,1:T(8,128)S(1)} %get-tuple-element.22), channel_id=1, source_target_pairs={{1,0},{2,1},{3,2},{4,3},{5,4},{6,5},{7,6},{0,7},{9,8},{10,9},{11,1... | collective-permute-start | bytes 294920 | tf_op jit(solution)/shard_map/ppermute | solution.py:16
  120.2 3.8 %fusion.63 = (f32[64,48,383]{2,0,1:T(8,128)S(1)}, f32[64,48,383]{2,0,1:T(8,128)}) fusion(f32[64,48,384]{2,0,1:T(8,128)S(1)} %get-tuple-element.6), kind=kLoop, calls=%fused_computation.91 | loop fusion | bytes 18825216 | tf_op jit(solution)/shard_map/slice | solution.py:22
  124.0 5.7 %bitcast_dynamic-update-slice_fusion.1 = bf16[6,64,48,384]{3,1,2,0:T(8,128)(2,1)} fusion(bf16[6,64,48,384]{3,1,2,0:T(8,128)(2,1)} %get-tuple-element.5, f32[64,48,384]{2,0,1:T(8,128)S(1)} %get-tuple-element.8, f32[64,48,383]{2,0,1:T(8,128)} %get-tuple-element.24, f32[64,48,383]{2,0,1:T(8,128)S(1)} %get-tuple-element.23, ...), kind=kLoop, calls=%fused_computation.34 | loop fusion | flops 9437184 | bytes 21417984 | tf_op jit(solution)/shard_map/stack | solution.py:48
  129.8 7.1 %fusion.23 = bf16[16,48,384]{2,0,1:T(8,128)(2,1)S(1)} fusion(bf16[6,64,48,384]{3,1,2,0:T(8,128)(2,1)} %bitcast_dynamic-update-slice_fusion.1, f32[16]{0:T(128)S(1)} %dynamic_slice.7, bf16[6,64,64]{2,1,0:T(8,128)(2,1)S(1)} %copy-done.3, s32[]{:T(128)S(6)} %select_n.4), kind=kOutput, calls=%fused_computation.42 | convolution fusion | flops 227082240 | bytes 14794820 | tf_op jit(solution)/shard_map/kio,kiyx->oyx/dot_general | solution.py:72
  136.8 0.9 copy.112
  (71 shorter events, 12.0 us)
Async XLA Ops:
  6.5 1.2 copy-start
  6.5 35.6 %all-gather.3.cloned.1.call-start = ((), (), s32[]{:S(2)}) async-start(), calls=%async_computation | async-start | bytes 1474560 | tf_op jit(solution)/shard_map/all_gather | solution.py:60
  43.6 4.0 %collective-permute-start = (f32[4,1,384]{2,0,1:T(4,128)S(1)}, f32[4,1,384]{2,0,1:T(4,128)S(1)}, u32[]{:S(2)}, u32[]{:S(2)}) collective-permute-start(f32[4,1,384]{2,0,1:T(4,128)S(1)} %get-tuple-element.57), channel_id=1, source_target_pairs={{0,1},{1,2},{2,3},{3,4},{4,5},{5,6},{6,7},{7,0},{8,9},{9,10},{10,1... | collective-permute-start | bytes 18440 | tf_op jit(solution)/shard_map/ppermute | solution.py:13
  43.7 4.0 %collective-permute-start.1 = (f32[4,1,384]{2,0,1:T(4,128)S(1)}, f32[4,1,384]{2,0,1:T(4,128)S(1)}, u32[]{:S(2)}, u32[]{:S(2)}) collective-permute-start(f32[4,1,384]{2,0,1:T(4,128)S(1)} %get-tuple-element.58), channel_id=1, source_target_pairs={{1,0},{2,1},{3,2},{4,3},{5,4},{6,5},{7,6},{0,7},{9,8},{10,9},{11,1... | collective-permute-start | bytes 18440 | tf_op jit(solution)/shard_map/ppermute | solution.py:16
  47.9 4.0 %collective-permute-start.2 = (f32[4,1,384]{2,0,1:T(4,128)S(1)}, f32[4,1,384]{2,0,1:T(4,128)S(1)}, u32[]{:S(2)}, u32[]{:S(2)}) collective-permute-start(f32[4,1,384]{2,0,1:T(4,128)S(1)} %get-tuple-element.53), channel_id=1, source_target_pairs={{0,1},{1,2},{2,3},{3,4},{4,5},{5,6},{6,7},{7,0},{8,9},{9,10},{10,1... | collective-permute-start | bytes 18440 | tf_op jit(solution)/shard_map/ppermute | solution.py:13
  48.6 3.4 %collective-permute-start.3 = (f32[4,1,384]{2,0,1:T(4,128)S(1)}, f32[4,1,384]{2,0,1:T(4,128)S(1)}, u32[]{:S(2)}, u32[]{:S(2)}) collective-permute-start(f32[4,1,384]{2,0,1:T(4,128)S(1)} %get-tuple-element.54), channel_id=1, source_target_pairs={{1,0},{2,1},{3,2},{4,3},{5,4},{6,5},{7,6},{0,7},{9,8},{10,9},{11,1... | collective-permute-start | bytes 18440 | tf_op jit(solution)/shard_map/ppermute | solution.py:16
  52.3 4.0 %collective-permute-start.4 = (f32[4,1,384]{2,0,1:T(4,128)S(1)}, f32[4,1,384]{2,0,1:T(4,128)S(1)}, u32[]{:S(2)}, u32[]{:S(2)}) collective-permute-start(f32[4,1,384]{2,0,1:T(4,128)S(1)} %get-tuple-element.49), channel_id=1, source_target_pairs={{0,1},{1,2},{2,3},{3,4},{4,5},{5,6},{6,7},{7,0},{8,9},{9,10},{10,1... | collective-permute-start | bytes 18440 | tf_op jit(solution)/shard_map/ppermute | solution.py:13
  52.8 3.6 %collective-permute-start.5 = (f32[4,1,384]{2,0,1:T(4,128)S(1)}, f32[4,1,384]{2,0,1:T(4,128)S(1)}, u32[]{:S(2)}, u32[]{:S(2)}) collective-permute-start(f32[4,1,384]{2,0,1:T(4,128)S(1)} %get-tuple-element.50), channel_id=1, source_target_pairs={{1,0},{2,1},{3,2},{4,3},{5,4},{6,5},{7,6},{0,7},{9,8},{10,9},{11,1... | collective-permute-start | bytes 18440 | tf_op jit(solution)/shard_map/ppermute | solution.py:16
  56.7 4.0 %collective-permute-start.6 = (f32[4,1,384]{2,0,1:T(4,128)S(1)}, f32[4,1,384]{2,0,1:T(4,128)S(1)}, u32[]{:S(2)}, u32[]{:S(2)}) collective-permute-start(f32[4,1,384]{2,0,1:T(4,128)S(1)} %get-tuple-element.45), channel_id=1, source_target_pairs={{0,1},{1,2},{2,3},{3,4},{4,5},{5,6},{6,7},{7,0},{8,9},{9,10},{10,1... | collective-permute-start | bytes 18440 | tf_op jit(solution)/shard_map/ppermute | solution.py:13
  57.1 12.5 %copy-start.4 = (bf16[6,4,64]{2,1,0:T(4,128)(2,1)S(1)}, bf16[6,4,64]{2,1,0:T(4,128)(2,1)}, u32[]{:S(2)}) copy-start(bf16[6,4,64]{2,1,0:T(4,128)(2,1)} %param.10) | copy-start | bytes 9220
  57.1 12.5 %copy-start.5 = (f32[64]{0:T(128)S(1)}, f32[64]{0:T(128)}, u32[]{:S(2)}) copy-start(f32[64]{0:T(128)} %param.11) | copy-start | bytes 772
  57.1 3.6 %collective-permute-start.7 = (f32[4,1,384]{2,0,1:T(4,128)S(1)}, f32[4,1,384]{2,0,1:T(4,128)S(1)}, u32[]{:S(2)}, u32[]{:S(2)}) collective-permute-start(f32[4,1,384]{2,0,1:T(4,128)S(1)} %get-tuple-element.46), channel_id=1, source_target_pairs={{1,0},{2,1},{3,2},{4,3},{5,4},{6,5},{7,6},{0,7},{9,8},{10,9},{11,1... | collective-permute-start | bytes 18440 | tf_op jit(solution)/shard_map/ppermute | solution.py:16
  61.0 4.0 %collective-permute-start.8 = (f32[4,1,384]{2,0,1:T(4,128)S(1)}, f32[4,1,384]{2,0,1:T(4,128)S(1)}, u32[]{:S(2)}, u32[]{:S(2)}) collective-permute-start(f32[4,1,384]{2,0,1:T(4,128)S(1)} %get-tuple-element.41), channel_id=1, source_target_pairs={{0,1},{1,2},{2,3},{3,4},{4,5},{5,6},{6,7},{7,0},{8,9},{9,10},{10,1... | collective-permute-start | bytes 18440 | tf_op jit(solution)/shard_map/ppermute | solution.py:13
  61.5 3.6 %collective-permute-start.9 = (f32[4,1,384]{2,0,1:T(4,128)S(1)}, f32[4,1,384]{2,0,1:T(4,128)S(1)}, u32[]{:S(2)}, u32[]{:S(2)}) collective-permute-start(f32[4,1,384]{2,0,1:T(4,128)S(1)} %get-tuple-element.42), channel_id=1, source_target_pairs={{1,0},{2,1},{3,2},{4,3},{5,4},{6,5},{7,6},{0,7},{9,8},{10,9},{11,1... | collective-permute-start | bytes 18440 | tf_op jit(solution)/shard_map/ppermute | solution.py:16
  72.0 1.4 copy-start.2
  72.7 5.4 %collective-permute-start.10 = (f32[64,1,384]{2,0,1:T(8,128)S(1)}, f32[64,1,384]{2,0,1:T(8,128)S(1)}, u32[]{:S(2)}, u32[]{:S(2)}) collective-permute-start(f32[64,1,384]{2,0,1:T(8,128)S(1)} %get-tuple-element.37), channel_id=1, source_target_pairs={{0,1},{1,2},{2,3},{3,4},{4,5},{5,6},{6,7},{7,0},{8,9},{9,10},{10,1... | collective-permute-start | bytes 294920 | tf_op jit(solution)/shard_map/ppermute | solution.py:13
  73.4 4.8 %collective-permute-start.11 = (f32[64,1,384]{2,0,1:T(8,128)S(1)}, f32[64,1,384]{2,0,1:T(8,128)S(1)}, u32[]{:S(2)}, u32[]{:S(2)}) collective-permute-start(f32[64,1,384]{2,0,1:T(8,128)S(1)} %get-tuple-element.38), channel_id=1, source_target_pairs={{1,0},{2,1},{3,2},{4,3},{5,4},{6,5},{7,6},{0,7},{9,8},{10,9},{11,1... | collective-permute-start | bytes 294920 | tf_op jit(solution)/shard_map/ppermute | solution.py:16
  82.0 5.5 %collective-permute-start.12 = (f32[64,1,384]{2,0,1:T(8,128)S(1)}, f32[64,1,384]{2,0,1:T(8,128)S(1)}, u32[]{:S(2)}, u32[]{:S(2)}) collective-permute-start(f32[64,1,384]{2,0,1:T(8,128)S(1)} %get-tuple-element.33), channel_id=1, source_target_pairs={{0,1},{1,2},{2,3},{3,4},{4,5},{5,6},{6,7},{7,0},{8,9},{9,10},{10,1... | collective-permute-start | bytes 294920 | tf_op jit(solution)/shard_map/ppermute | solution.py:13
  82.3 5.1 %collective-permute-start.13 = (f32[64,1,384]{2,0,1:T(8,128)S(1)}, f32[64,1,384]{2,0,1:T(8,128)S(1)}, u32[]{:S(2)}, u32[]{:S(2)}) collective-permute-start(f32[64,1,384]{2,0,1:T(8,128)S(1)} %get-tuple-element.34), channel_id=1, source_target_pairs={{1,0},{2,1},{3,2},{4,3},{5,4},{6,5},{7,6},{0,7},{9,8},{10,9},{11,1... | collective-permute-start | bytes 294920 | tf_op jit(solution)/shard_map/ppermute | solution.py:16
  92.7 6.5 %collective-permute-start.14 = (f32[64,1,384]{2,0,1:T(8,128)S(1)}, f32[64,1,384]{2,0,1:T(8,128)S(1)}, u32[]{:S(2)}, u32[]{:S(2)}) collective-permute-start(f32[64,1,384]{2,0,1:T(8,128)S(1)} %get-tuple-element.29), channel_id=1, source_target_pairs={{0,1},{1,2},{2,3},{3,4},{4,5},{5,6},{6,7},{7,0},{8,9},{9,10},{10,1... | collective-permute-start | bytes 294920 | tf_op jit(solution)/shard_map/ppermute | solution.py:13
  93.2 6.0 %collective-permute-start.15 = (f32[64,1,384]{2,0,1:T(8,128)S(1)}, f32[64,1,384]{2,0,1:T(8,128)S(1)}, u32[]{:S(2)}, u32[]{:S(2)}) collective-permute-start(f32[64,1,384]{2,0,1:T(8,128)S(1)} %get-tuple-element.30), channel_id=1, source_target_pairs={{1,0},{2,1},{3,2},{4,3},{5,4},{6,5},{7,6},{0,7},{9,8},{10,9},{11,1... | collective-permute-start | bytes 294920 | tf_op jit(solution)/shard_map/ppermute | solution.py:16
  105.2 6.5 %collective-permute-start.16 = (f32[64,1,384]{2,0,1:T(8,128)S(1)}, f32[64,1,384]{2,0,1:T(8,128)S(1)}, u32[]{:S(2)}, u32[]{:S(2)}) collective-permute-start(f32[64,1,384]{2,0,1:T(8,128)S(1)} %get-tuple-element.25), channel_id=1, source_target_pairs={{0,1},{1,2},{2,3},{3,4},{4,5},{5,6},{6,7},{7,0},{8,9},{9,10},{10,1... | collective-permute-start | bytes 294920 | tf_op jit(solution)/shard_map/ppermute | solution.py:13
  105.2 6.4 %collective-permute-start.17 = (f32[64,1,384]{2,0,1:T(8,128)S(1)}, f32[64,1,384]{2,0,1:T(8,128)S(1)}, u32[]{:S(2)}, u32[]{:S(2)}) collective-permute-start(f32[64,1,384]{2,0,1:T(8,128)S(1)} %get-tuple-element.26), channel_id=1, source_target_pairs={{1,0},{2,1},{3,2},{4,3},{5,4},{6,5},{7,6},{0,7},{9,8},{10,9},{11,1... | collective-permute-start | bytes 294920 | tf_op jit(solution)/shard_map/ppermute | solution.py:16
  117.5 6.5 %collective-permute-start.18 = (f32[64,1,384]{2,0,1:T(8,128)S(1)}, f32[64,1,384]{2,0,1:T(8,128)S(1)}, u32[]{:S(2)}, u32[]{:S(2)}) collective-permute-start(f32[64,1,384]{2,0,1:T(8,128)S(1)} %get-tuple-element.21), channel_id=1, source_target_pairs={{0,1},{1,2},{2,3},{3,4},{4,5},{5,6},{6,7},{7,0},{8,9},{9,10},{10,1... | collective-permute-start | bytes 294920 | tf_op jit(solution)/shard_map/ppermute | solution.py:13
  117.6 6.4 %collective-permute-start.19 = (f32[64,1,384]{2,0,1:T(8,128)S(1)}, f32[64,1,384]{2,0,1:T(8,128)S(1)}, u32[]{:S(2)}, u32[]{:S(2)}) collective-permute-start(f32[64,1,384]{2,0,1:T(8,128)S(1)} %get-tuple-element.22), channel_id=1, source_target_pairs={{1,0},{2,1},{3,2},{4,3},{5,4},{6,5},{7,6},{0,7},{9,8},{10,9},{11,1... | collective-permute-start | bytes 294920 | tf_op jit(solution)/shard_map/ppermute | solution.py:16
  124.0 5.8 %copy-start.3 = (bf16[6,64,64]{2,1,0:T(8,128)(2,1)S(1)}, bf16[6,64,64]{2,1,0:T(8,128)(2,1)}, u32[]{:S(2)}) copy-start(bf16[6,64,64]{2,1,0:T(8,128)(2,1)} %param.12) | copy-start | bytes 147460
  124.0 13.7 %copy-start.1 = (bf16[25,48,384]{2,1,0:T(8,128)(2,1)S(1)}, bf16[25,48,384]{2,1,0:T(8,128)(2,1)}, u32[]{:S(2)}) copy-start(bf16[25,48,384]{2,1,0:T(8,128)(2,1)} %param.7) | copy-start | bytes 2764804
Sparse Core Ops, SparseCore 0:
  8.9 33.1 all-gather.2
